TPU v7x, 32 devices: a whole 2x2x4 slice. The times are simulated.
32 devices in a mesh: rep: 2 (over x), node: 2 (over core), local: 8 (over z, y).
Axes of the slice: x: 2, y: 2, z: 4, core: 2. Of those that a mesh axis runs over, the one named last changes fastest.
Arguments:
- head_outputs: bfloat16 [8192, 2560], P(('rep', 'node', 'local')), parts along dimension 0, may hold values from -6 to 6
- out_grads: bfloat16 [8192, 2560], P(('rep', 'node', 'local')), parts along dimension 0, may hold values from -6 to 6
- quant_values: bfloat16 [2560, 2560], P(('node', 'local')), may hold values from -0.125 to 0.125
- block_scales: bfloat16 [2560, 10], P(('node', 'local')), may hold values from 0.5 to 2
Outputs:
- projected: bfloat16 [8192, 2560], P(('rep', 'node', 'local')), parts along dimension 0
- head_grads: bfloat16 [8192, 2560], P(('rep', 'node', 'local')), parts along dimension 0
- weight_grad: float32 [5120, 2560], P(('rep', 'node', 'local')), parts along dimension 0
There are 2 independent parts, one for each index of `rep`. A program takes and returns all parts, laid end to end along the dimension named above; an argument that names none is the same for every part. Nothing has to cross between parts.
All inputs are finite; a program needn't handle non-finite values.
Results may differ from a plain program's by a relative error of at most 0.005.
Values may be sent and summed in bfloat16 or wider, within the bound.
A program may use at most 192 MiB of HBM per device.

v0:
```python
import jax
import jax.numpy as jnp
from jax import lax
from jax.sharding import PartitionSpec as P


def dequantize(values, scales):
    row_count = values.shape[0]
    col_count = values.shape[1]
    blocks = scales.shape[1]
    widened = values.astype(jnp.float32).reshape(row_count, blocks, col_count // blocks)
    widened = widened * scales.astype(jnp.float32)[:, :, None]
    return widened.reshape(row_count, col_count).astype(jnp.bfloat16)


def fetch_weights(quant_values, block_scales):
    whole = (
        lax.all_gather(quant_values, ("node", "local"), axis=0, tiled=True),
        lax.all_gather(block_scales, ("node", "local"), axis=0, tiled=True),
    )
    values_all = whole[0]
    scales_all = whole[1]
    return dequantize(values_all, scales_all)


def apply_weight(weight, head_outputs, out_grads):
    projected = jnp.dot(head_outputs, weight, preferred_element_type=jnp.float32).astype(
        jnp.bfloat16
    )
    head_grads = lax.dot_general(
        out_grads, weight, (((1,), (1,)), ((), ())), preferred_element_type=jnp.float32
    ).astype(jnp.bfloat16)
    return (projected, head_grads)


def reduce_grads(head_outputs, out_grads, node_count, local_count):
    partial_value = lax.dot_general(
        head_outputs, out_grads, (((0,), (0,)), ((), ())), preferred_element_type=jnp.float32
    ).astype(jnp.bfloat16)
    col_count = partial_value.shape[1]
    shaped = partial_value.reshape(node_count, local_count, -1, col_count)
    arrived = lax.all_to_all(shaped, "local", split_axis=1, concat_axis=1, tiled=True)
    group_sum = jnp.sum(arrived, axis=1, dtype=jnp.float32)
    second = lax.all_to_all(group_sum, "node", split_axis=0, concat_axis=0, tiled=True)
    return jnp.sum(second, axis=0)


def per_device(head_outputs, out_grads, quant_values, block_scales):
    node_count = lax.axis_size("node")
    local_count = lax.axis_size("local")
    token_count = head_outputs.shape[0] * node_count * local_count
    weight = fetch_weights(quant_values, block_scales)
    projected, head_grads = apply_weight(weight, head_outputs, out_grads)
    reduced = reduce_grads(head_outputs, out_grads, node_count, local_count)
    return (projected, head_grads, reduced * token_count ** (-0.5))


def solution(mesh):
    return jax.shard_map(
        per_device,
        mesh=mesh,
        in_specs=(
            P(("rep", "node", "local"), None),
            P(("rep", "node", "local"), None),
            P(("node", "local"), None),
            P(("node", "local"), None),
        ),
        out_specs=(
            P(("rep", "node", "local"), None),
            P(("rep", "node", "local"), None),
            P(("rep", "node", "local"), None),
        ),
        check_vma=False,
    )
```

profile of v0, /device:TPU:0, one launch (start us, length us, event | category | flops | bytes accessed | tf_op | source)
XLA Modules:
  0.0 475.8 jit_solution(11641189069028659097)
XLA Ops:
  7.2 0.0 copy-start
  7.2 0.0 all-gather.3.cloned.1.call-start
  7.2 0.7 all-gather.3.cloned.1.call-update
  7.9 0.6 copy-done
  8.5 5.2 %convolution_convert_fusion = bf16[2560,2560]{1,0:T(8,128)(2,1)S(1)} fusion(bf16[256,2560]{1,0:T(8,128)(2,1)} %param.4, bf16[256,2560]{1,0:T(8,128)(2,1)S(1)} %copy-done), kind=kOutput, calls=%fused_computation.3 | convolution fusion | flops 3361996800 | bytes 15728640 | tf_op jit(solution)/shard_map/dot_general | solution.py:37
  13.7 5.8 %copy.25 = bf16[2,8,160,2560]{3,2,0,1:T(8,128)(2,1)} copy(bf16[2,8,160,2560]{3,2,1,0:T(8,128)(2,1)S(1)} %bitcast.18) | data formatting | bytes 26214400 | tf_op jit(solution)/shard_map/reshape | solution.py:41
  19.4 0.0 copy-start.2
  19.4 7.4 %all-to-all-start = ((bf16[2,8,160,2560]{3,2,0,1:T(8,128)(2,1)}), bf16[2,8,160,2560]{3,2,0,1:T(8,128)(2,1)}, u32[]{:S(2)}, u32[]{:S(2)}) async-start(bf16[2,8,160,2560]{3,2,0,1:T(8,128)(2,1)} %copy.25), calls=%async_computation | async-start | bytes 26214400 | tf_op jit(solution)/shard_map/all_to_all | solution.py:42
  26.9 0.0 copy-done.2
  26.9 381.6 %all-gather = bf16[16,160,10]{1,2,0:T(8,128)(2,1)S(1)} all-gather(bf16[1,160,10]{1,2,0:T(8,128)(2,1)S(1)} %bitcast.19), channel_id=1, replica_groups=mesh['rep'=2,'node'=2,'local'=8] {'node','local'}, dimensions={0}, use_global_device_ids=true | all-gather | bytes 54400 | tf_op jit(solution)/shard_map/all_gather | solution.py:19
  408.5 0.1 reshape.16
  408.6 0.0 all-to-all-done
  408.6 8.6 %convert_reduce_fusion = f32[2,160,2560]{2,1,0:T(8,128)} fusion(bf16[2,8,160,2560]{3,2,0,1:T(8,128)(2,1)} %all-to-all-done), kind=kLoop, calls=%fused_computation.2 | loop fusion | flops 12288000 | bytes 16384000 | tf_op jit(solution)/shard_map/reduce_sum | solution.py:43
  417.2 10.5 %all_to_all.10 = f32[2,160,2560]{2,1,0:T(8,128)} all-to-all(f32[2,160,2560]{2,1,0:T(8,128)} %convert_reduce_fusion), channel_id=1, replica_groups=mesh['rep'=2,'node'=2,'local'=8] {'node'}, dimensions={0} | all-to-all | bytes 6553600 | tf_op jit(solution)/shard_map/all_to_all | solution.py:44
  427.6 2.3 reduce_sum.19
  430.0 1.3 broadcast_multiply_fusion
  431.2 0.0 all-gather.3.cloned.1.call-done
  431.2 17.6 %copy.23 = bf16[2560,2560]{0,1:T(8,128)(2,1)} copy(bf16[2560,2560]{1,0:T(8,128)(2,1)} %all-gather.3.cloned.1.call-done) | data formatting | bytes 26214400 | tf_op jit(solution)/shard_map/all_gather | solution.py:18
  448.9 7.8 %fusion = bf16[2560,2560]{0,1:T(8,128)(2,1)S(1)} fusion(bf16[2560,2560]{0,1:T(8,128)(2,1)} %copy.23, f32[2560,10]{0,1:T(8,128)S(1)} %reshape.16), kind=kLoop, calls=%fused_computation.1 | loop fusion | flops 19660800 | bytes 26316800 | tf_op jit(solution)/shard_map/convert_element_type | solution.py:13
  456.6 0.0 copy-start.1
  456.7 3.6 fusion.1
  460.3 0.0 copy-done.1
  460.3 4.7 fusion.2
  464.9 2.4 copy.26
  467.4 1.6 copy.27
  (1 shorter events, 0.0 us)
Async XLA Ops:
  7.2 1.3 copy-start
  7.2 424.1 %all-gather.3.cloned.1.call-start = ((), (), s32[]{:S(2)}) async-start(), calls=%async_computation.2 | async-start | bytes 13926400 | tf_op jit(solution)/shard_map/all_gather | solution.py:18
  19.4 7.4 %copy-start.2 = (bf16[160,10]{0,1:T(8,128)(2,1)S(1)}, bf16[160,10]{0,1:T(8,128)(2,1)}, u32[]{:S(2)}) copy-start(bf16[160,10]{0,1:T(8,128)(2,1)} %param.7) | copy-start | bytes 9604
  19.4 389.2 %all-to-all-start = ((bf16[2,8,160,2560]{3,2,0,1:T(8,128)(2,1)}), bf16[2,8,160,2560]{3,2,0,1:T(8,128)(2,1)}, u32[]{:S(2)}, u32[]{:S(2)}) async-start(bf16[2,8,160,2560]{3,2,0,1:T(8,128)(2,1)} %copy.25), calls=%async_computation | async-start | bytes 26214400 | tf_op jit(solution)/shard_map/all_to_all | solution.py:42
  456.6 3.6 copy-start.1
Sparse Core Ops, SparseCore 0:
  10.2 316.8 all-gather.2
where the time goes:
time: 477 us; the launch traced here: 476 us
  blocking collectives  392 us (82%)
  local copies, waits for them, and re-layouts  28.1 us (6%)
  other arithmetic  19.9 us (4%)
  between operations  14.1 us (3%)
  matrix products  13.5 us (3%)
  starting transfers between devices  7.45 us (2%)
    all_gather x1, blocking collectives, fetch_weights(): lax.all_gather(block_scales, ('node', 'local'), axis=0, tiled=True)  382 us
    all_gather x1, local copies, waits for them, and re-layouts, fetch_weights(): lax.all_gather(quant_values, ('node', 'local'), axis=0, tiled=True)  17.6 us
    all_to_all x1, blocking collectives, reduce_grads(): lax.all_to_all(group_sum, 'node', split_axis=0, concat_axis=0, tiled=True)  10.5 us
  transfers between devices with their start and end apart: 2, of which 0 were waited for; matrix products, arithmetic and copies ran while one was open for 5% of the time, Pallas kernels for 0%

commit v1 on v0

--- a/solution.py
+++ b/solution.py
@@ -1,6 +1,10 @@
+import functools
+
 import jax
 import jax.numpy as jnp
 from jax import lax
+from jax.experimental import pallas as pl
+from jax.experimental.pallas import tpu as pltpu
 from jax.sharding import PartitionSpec as P
 
 
@@ -45,7 +49,322 @@
     return jnp.sum(second, axis=0)
 
 
-def per_device(head_outputs, out_grads, quant_values, block_scales):
+MESH = pl.DeviceIdType.MESH
+CHUNKS = 4
+
+
+def fused_kernel(
+    scale, ho_ref, og_ref, ht_ref, qv_ref, sc_ref, proj_ref, hg_ref, wg_ref,
+    w, htall, ogall, gsum, sbuf, f0, f1, ibuf, acc,
+    hts, htr, ogys, ogyr, ogcs, ogcr, ogds, ogdr,
+    wr, zs, ys, xs, cs, rss, f0r, f1r, ir,
+):
+    x = lax.axis_index("rep")
+    c = lax.axis_index("node")
+    l = lax.axis_index("local")
+    z = l // 2
+    y = l % 2
+    xn, yn, cn = 1 - x, 1 - y, 1 - c
+    side = z // 2
+    pair = z + 1 - 2 * (z % 2)
+    inner = 2 - side
+    outer = 3 * (1 - side)
+    is_inner = (z == 1) | (z == 2)
+    shard = qv_ref.shape[0]
+    half = shard // 2
+    tok = ho_ref.shape[0]
+    cols = og_ref.shape[1]
+    cw = cols // CHUNKS
+
+    def dev(xx, cc, zz, yy):
+        return (xx, cc, zz * 2 + yy)
+
+    to_x = dev(xn, c, z, y)
+    to_y = dev(x, c, z, yn)
+    to_c = dev(x, cn, z, y)
+    to_d = dev(x, cn, z, yn)
+    to_pair = dev(x, c, pair, y)
+    to_inner = dev(x, c, inner, y)
+    to_outer = dev(x, c, outer, y)
+
+    barrier = pltpu.get_barrier_semaphore()
+    for other in (to_x, to_y, to_c, to_d, to_pair, to_inner, to_outer):
+        pl.semaphore_signal(barrier, inc=1, device_id=other, device_id_type=MESH)
+    pl.semaphore_wait(barrier, 7)
+
+    def rcopy(src, dst, ssem, rsem, to):
+        return pltpu.make_async_remote_copy(
+            src_ref=src, dst_ref=dst, send_sem=ssem, recv_sem=rsem,
+            device_id=to, device_id_type=MESH,
+        )
+
+    def piece(zz, yy, hh, cc, ssem, to):
+        row = pl.multiple_of(((cc * 8 + zz * 2 + yy) * 2 + hh) * half, half)
+        at = w.at[pl.ds(row, half), :]
+        return rcopy(at, at, ssem, wr.at[((cc * 4 + zz) * 2 + yy) * 2 + hh], to)
+
+    started = []
+
+    def send(copy):
+        copy.start()
+        started.append(copy)
+
+    inner_started = []
+
+    def arrive(zz, yy, hh, cc, sem, frm):
+        piece(zz, yy, hh, cc, sem, frm).wait_recv()
+
+    n_c = [0]
+
+    def core_send(zz, yy, hh):
+        send(piece(zz, yy, hh, c, cs.at[n_c[0]], to_c))
+        n_c[0] += 1
+
+    n_x = [0]
+
+    def x_send(zz, yy):
+        send(piece(zz, yy, x, c, xs.at[n_x[0]], to_x))
+        n_x[0] += 1
+
+    n_y = [0]
+
+    def y_send(zz):
+        send(piece(zz, y, x, c, ys.at[n_y[0]], to_y))
+        n_y[0] += 1
+
+    htc = {}
+    for k, to, cc, yy in ((2, to_y, c, yn), (3, to_d, cn, yn), (1, to_c, cn, y)):
+        htc[k] = rcopy(
+            ht_ref.at[cc, yy], htall.at[:, pl.ds(k * tok, tok)], hts.at[k - 1], htr.at[k - 1], to
+        )
+        send(htc[k])
+
+    ogall[0, 0:tok, :] = og_ref[:, 0:cw]
+
+    def ogy(ch):
+        return rcopy(
+            ogall.at[ch, pl.ds(0, tok), :], ogall.at[ch, pl.ds(2 * tok, tok), :],
+            ogys.at[ch], ogyr.at[ch], to_y,
+        )
+
+    def ogc(ch):
+        return rcopy(
+            ogall.at[ch, pl.ds(0, tok), :], ogall.at[ch, pl.ds(tok, tok), :],
+            ogcs.at[ch], ogcr.at[ch], to_c,
+        )
+
+    def ogd(ch):
+        return rcopy(
+            ogall.at[ch, pl.ds(2 * tok, tok), :], ogall.at[ch, pl.ds(3 * tok, tok), :],
+            ogds.at[ch], ogdr.at[ch], to_c,
+        )
+
+    send(ogy(0))
+
+    own = pl.multiple_of((c * 8 + l) * shard, shard)
+    qb = cols // sc_ref.shape[1]
+    for b in range(sc_ref.shape[1]):
+        w[pl.ds(own, shard), b * qb:(b + 1) * qb] = (
+            qv_ref[:, b * qb:(b + 1) * qb].astype(jnp.float32)
+            * sc_ref[:, b:b + 1].astype(jnp.float32)
+        ).astype(jnp.bfloat16)
+
+    send(piece(z, y, x, c, zs.at[0], to_pair))
+
+    @pl.when(is_inner)
+    def _():
+        cp = piece(z, y, x, c, zs.at[1], to_inner)
+        cp.start()
+        inner_started.append(cp)
+
+    for ch in range(1, CHUNKS):
+        ogall[ch, 0:tok, :] = og_ref[:, ch * cw:(ch + 1) * cw]
+    send(ogy(1))
+    for ch in range(CHUNKS):
+        send(ogc(ch))
+    htall[:, 0:tok] = ht_ref[c, y]
+    core_send(z, y, 0)
+    core_send(z, y, 1)
+
+    def z_step(zz, sem, to):
+        arrive(zz, y, x, c, zs.at[0], to_pair)
+
+        @pl.when(is_inner)
+        def _():
+            piece(zz, y, x, c, zs.at[sem], to).start()
+
+        x_send(zz, y)
+        core_send(zz, y, x)
+
+    def grads(ch):
+        ogy(ch).wait_recv()
+        send(ogd(ch))
+        if ch + 2 < CHUNKS:
+            send(ogy(ch + 2))
+        if ch == 0:
+            for k in (1, 2, 3):
+                htc[k].wait_recv()
+        ogc(ch).wait_recv()
+        ogd(ch).wait_recv()
+        term = jnp.dot(htall[...], ogall[ch], preferred_element_type=jnp.float32)
+        gsum[ch] = term.reshape(4, shard, cw)
+        sbuf[ch, 0] = gsum[ch, pair].astype(jnp.bfloat16)
+        send(rcopy(sbuf.at[ch, 0], f0.at[ch], rss.at[ch, 0], f0r.at[ch], to_pair))
+
+        @pl.when(jnp.logical_not(is_inner))
+        def _():
+            for j, zz in ((1, inner), (2, outer)):
+                sbuf[ch, j] = gsum[ch, zz].astype(jnp.bfloat16)
+                rcopy(sbuf.at[ch, j], ibuf.at[ch, j - 1], rss.at[ch, j], ir.at[ch, j - 1], to_pair).start()
+
+    def passed_on(ch):
+        @pl.when(is_inner)
+        def _():
+            for j, zz, to in ((2, outer, to_outer), (1, inner, to_inner)):
+                rcopy(sbuf.at[ch, j], ibuf.at[ch, j - 1], rss.at[ch, j], ir.at[ch, j - 1], to_pair).wait_recv()
+                sbuf[ch, j] = (gsum[ch, zz] + ibuf[ch, j - 1].astype(jnp.float32)).astype(jnp.bfloat16)
+                rcopy(sbuf.at[ch, j], f1.at[ch], rss.at[ch, j], f1r.at[ch], to).start()
+
+    def finish(ch):
+        rcopy(sbuf.at[ch, 0], f0.at[ch], rss.at[ch, 0], f0r.at[ch], to_pair).wait_recv()
+        rcopy(sbuf.at[ch, 0], f1.at[ch], rss.at[ch, 0], f1r.at[ch], to_pair).wait_recv()
+        wg_ref[:, ch * cw:(ch + 1) * cw] = (
+            gsum[ch, z] + f0[ch].astype(jnp.float32) + f1[ch].astype(jnp.float32)
+        ) * scale
+
+    quarter = 4 * shard
+    tile = cw
+
+    def apply(cc, ss, first):
+        row = pl.multiple_of((cc * 2 + ss) * quarter, 128)
+        left = ho_ref[:, pl.ds(row, quarter)]
+
+        def body(t, carry):
+            at = pl.ds(pl.multiple_of(t * tile, 128), tile)
+            term = jnp.dot(left, w[pl.ds(row, quarter), at], preferred_element_type=jnp.float32)
+            if first:
+                acc[:, at] = term
+            else:
+                acc[:, at] += term
+            return carry
+
+        lax.fori_loop(0, cols // tile, body, 0)
+        hg_ref[:, pl.ds(row, quarter)] = lax.dot_general(
+            og_ref[...], w[pl.ds(row, quarter), :], (((1,), (1,)), ((), ())),
+            preferred_element_type=jnp.float32,
+        ).astype(jnp.bfloat16)
+
+    def b_step(zz):
+        arrive(zz, yn, x, c, ys.at[0], to_y)
+        x_send(zz, yn)
+        core_send(zz, yn, x)
+
+    def c_step(zz, yy):
+        arrive(zz, yy, xn, c, xs.at[0], to_x)
+        core_send(zz, yy, xn)
+
+    def core_arrive(zz):
+        for yy in (0, 1):
+            for hh in (0, 1):
+                arrive(zz, yy, hh, cn, cs.at[0], to_c)
+
+    z_step(pair, 2, to_inner)
+    z_step(inner, 3, to_pair)
+    grads(0)
+    z_step(outer, 4, to_pair)
+    grads(1)
+    passed_on(0)
+    grads(2)
+    y_send(z)
+    y_send(pair)
+    passed_on(1)
+    grads(3)
+    y_send(inner)
+    y_send(outer)
+    passed_on(2)
+    c_step(pair, y)
+    c_step(inner, y)
+    c_step(outer, y)
+    b_step(z)
+    passed_on(3)
+    b_step(pair)
+    c_step(z, yn)
+    b_step(inner)
+    c_step(pair, yn)
+    b_step(outer)
+    apply(c, side, True)
+    core_arrive(z)
+    core_arrive(pair)
+    apply(cn, side, False)
+    c_step(inner, yn)
+    c_step(outer, yn)
+    for ch in range(CHUNKS):
+        finish(ch)
+    apply(c, 1 - side, False)
+    core_arrive(inner)
+    core_arrive(outer)
+    apply(cn, 1 - side, False)
+    proj_ref[...] = acc[...].astype(jnp.bfloat16)
+
+    for copy in started:
+        copy.wait_send()
+    for ch in range(CHUNKS):
+        for j in (1, 2):
+            rcopy(sbuf.at[ch, j], f1.at[ch], rss.at[ch, j], f1r.at[ch], to_pair).wait_send()
+
+    @pl.when(is_inner)
+    def _():
+        for k, zz in ((1, z), (2, pair), (3, inner), (4, outer)):
+            piece(zz, y, x, c, zs.at[k], to_pair).wait_send()
+
+
+def per_device_fused(head_outputs, out_grads, quant_values, block_scales):
+    tok, rows = head_outputs.shape
+    cols = out_grads.shape[1]
+    shard = quant_values.shape[0]
+    cw = cols // CHUNKS
+    token_count = tok * lax.axis_size("node") * lax.axis_size("local")
+    turned = head_outputs.T.reshape(2, 4, 2, shard, tok).transpose(0, 2, 1, 3, 4)
+    turned = turned.reshape(2, 2, 4 * shard, tok)
+    vmem = pl.BlockSpec(memory_space=pltpu.VMEM)
+    bf16, f32 = jnp.bfloat16, jnp.float32
+    dma = pltpu.SemaphoreType.DMA
+    return pl.pallas_call(
+        functools.partial(fused_kernel, token_count ** (-0.5)),
+        out_shape=(
+            jax.ShapeDtypeStruct((tok, cols), bf16),
+            jax.ShapeDtypeStruct((tok, rows), bf16),
+            jax.ShapeDtypeStruct((shard, cols), f32),
+        ),
+        in_specs=[vmem] * 5,
+        out_specs=(vmem,) * 3,
+        scratch_shapes=[
+            pltpu.VMEM((rows, cols), bf16),
+            pltpu.VMEM((4 * shard, 4 * tok), bf16),
+            pltpu.VMEM((CHUNKS, 4 * tok, cw), bf16),
+            pltpu.VMEM((CHUNKS, 4, shard, cw), f32),
+            pltpu.VMEM((CHUNKS, 3, shard, cw), bf16),
+            pltpu.VMEM((CHUNKS, shard, cw), bf16),
+            pltpu.VMEM((CHUNKS, shard, cw), bf16),
+            pltpu.VMEM((CHUNKS, 2, shard, cw), bf16),
+            pltpu.VMEM((tok, cols), f32),
+            dma((3,)), dma((3,)),
+            dma((CHUNKS,)), dma((CHUNKS,)),
+            dma((CHUNKS,)), dma((CHUNKS,)),
+            dma((CHUNKS,)), dma((CHUNKS,)),
+            dma((32,)), dma((5,)), dma((4,)), dma((7,)), dma((16,)),
+            dma((CHUNKS, 3)), dma((CHUNKS,)), dma((CHUNKS,)), dma((CHUNKS, 2)),
+        ],
+        compiler_params=pltpu.CompilerParams(
+            collective_id=0, has_side_effects=True, vmem_limit_bytes=60 * 1024 * 1024
+        ),
+        cost_estimate=pl.CostEstimate(
+            flops=6 * tok * rows * cols, bytes_accessed=8 * tok * cols, transcendentals=0
+        ),
+    )(head_outputs, out_grads, turned, quant_values, block_scales)
+
+
+def per_device_plain(head_outputs, out_grads, quant_values, block_scales):
     node_count = lax.axis_size("node")
     local_count = lax.axis_size("local")
     token_count = head_outputs.shape[0] * node_count * local_count
@@ -53,6 +372,24 @@
     projected, head_grads = apply_weight(weight, head_outputs, out_grads)
     reduced = reduce_grads(head_outputs, out_grads, node_count, local_count)
     return (projected, head_grads, reduced * token_count ** (-0.5))
+
+
+def per_device(head_outputs, out_grads, quant_values, block_scales):
+    node_count = lax.axis_size("node")
+    local_count = lax.axis_size("local")
+    shard = quant_values.shape[0]
+    fits = (
+        lax.axis_size("rep") == 2
+        and node_count == 2
+        and local_count == 8
+        and shard % 32 == 0
+        and (4 * shard) % 128 == 0
+        and head_outputs.shape[0] % 256 == 0
+        and out_grads.shape[1] % (CHUNKS * 128) == 0
+    )
+    if fits:
+        return per_device_fused(head_outputs, out_grads, quant_values, block_scales)
+    return per_device_plain(head_outputs, out_grads, quant_values, block_scales)
 
 
 def solution(mesh):

time: 477 us -> 138 us (0.29)
  the two profiles are of different devices: /device:TPU:0 before, /device:TPU:8 now
where the time goes in v1:
time: 138 us; the launch traced here: 137 us
  Pallas kernels  127 us (92%)
  local copies, waits for them, and re-layouts  9.79 us (7%)
    pallas_call x1, Pallas kernels, per_device_fused(): pl.pallas_call(functools.partial(fused_kernel, token_count ** (-0.5)), ou...  127 us
    unnamed x9, local copies, waits for them, and re-layouts  8.65 us

profile of v1, /device:TPU:8, one launch (start us, length us, event | category | flops | bytes accessed | tf_op | source)
XLA Modules:
  0.0 137.4 jit_solution(658256608996954103)
XLA Ops:
  0.6 1.4 %copy.11.sc_ref = bf16[160,10]{1,0:T(8,128)(2,1)} copy(bf16[160,10]{0,1:T(8,128)(2,1)} %param.7) | data formatting | bytes 6400 | tf_op args[3]
  2.1 1.6 %copy.9 = bf16[256,2560]{0,1:T(8,128)(2,1)S(1)} copy(bf16[256,2560]{1,0:T(8,128)(2,1)} %ho_ref.1) | data formatting | bytes 2621440 | tf_op args[0]
  3.7 1.1 copy.10
  4.8 127.0 %shard_map.67 = (bf16[256,2560]{1,0:T(8,128)(2,1)}, bf16[256,2560]{1,0:T(8,128)(2,1)}, f32[160,2560]{1,0:T(8,128)}) custom-call(bf16[256,2560]{1,0:T(8,128)(2,1)} %ho_ref.1, bf16[256,2560]{1,0:T(8,128)(2,1)} %og_ref.1, bf16[2,2,640,256]{3,2,1,0:T(8,128)(2,1)} %bitcast.7, bf16[160,2560]{1,0:T(8,128)(2,1)} %qv_ref.1, bf16[160,10]{1,0:T(8,128)(2,1)} %copy.11.sc_ref), custom_call_target="tpu_custom_call" | custom-call | flops 10066329600 | bytes 5242880 | tf_op jit(solution)/shard_map/pallas_call | solution.py:332
  131.8 0.0 copy-start.1
  131.8 2.6 %copy.15 = bf16[256,2560]{1,0:T(8,128)(2,1)} copy(bf16[256,2560]{1,0:T(8,128)(2,1)} %get-tuple-element.6) | data formatting | bytes 2621440
  134.4 0.0 copy-done.1
  134.4 0.0 copy-start
  134.4 1.1 copy.16
  135.4 0.8 copy-done
  136.3 1.2 copy.17
Async XLA Ops:
  131.8 2.6 %copy-start.1 = (bf16[256,2560]{1,0:T(8,128)(2,1)S(1)}, bf16[256,2560]{1,0:T(8,128)(2,1)}, u32[]{:S(2)}) copy-start(bf16[256,2560]{1,0:T(8,128)(2,1)} %get-tuple-element.7) | copy-start | bytes 3932164
  134.4 1.9 %copy-start = (f32[160,2560]{1,0:T(8,128)S(1)}, f32[160,2560]{1,0:T(8,128)}, u32[]{:S(2)}) copy-start(f32[160,2560]{1,0:T(8,128)} %get-tuple-element.8) | copy-start | bytes 4915204

commit v2 on v1

--- a/solution.py
+++ b/solution.py
@@ -54,8 +54,8 @@
 
 
 def fused_kernel(
-    scale, ho_ref, og_ref, ht_ref, qv_ref, sc_ref, proj_ref, hg_ref, wg_ref,
-    w, htall, ogall, gsum, sbuf, f0, f1, ibuf, acc,
+    scale, ho_ref, og_ref, qv_ref, sc_ref, proj_ref, hg_ref, wg_ref,
+    w, turned, htall, ogall, gsum, sbuf, f0, f1, ibuf, acc,
     hts, htr, ogys, ogyr, ogcs, ogcr, ogds, ogdr,
     wr, zs, ys, xs, cs, rss, f0r, f1r, ir,
 ):
@@ -132,13 +132,6 @@
         send(piece(zz, y, x, c, ys.at[n_y[0]], to_y))
         n_y[0] += 1
 
-    htc = {}
-    for k, to, cc, yy in ((2, to_y, c, yn), (3, to_d, cn, yn), (1, to_c, cn, y)):
-        htc[k] = rcopy(
-            ht_ref.at[cc, yy], htall.at[:, pl.ds(k * tok, tok)], hts.at[k - 1], htr.at[k - 1], to
-        )
-        send(htc[k])
-
     ogall[0, 0:tok, :] = og_ref[:, 0:cw]
 
     def ogy(ch):
@@ -160,6 +153,23 @@
         )
 
     send(ogy(0))
+
+    step = 256
+    for b in range(ho_ref.shape[1] // step):
+        turned[b * step:(b + 1) * step, :] = ho_ref[:, b * step:(b + 1) * step].T
+
+    def ht_rows(cc, zz, yy):
+        return pl.ds(pl.multiple_of((cc * 8 + zz * 2 + yy) * shard, shard), shard)
+
+    htc = []
+    for k, to, cc, yy in ((2, to_y, c, yn), (3, to_d, cn, yn), (1, to_c, cn, y)):
+        for zz in range(4):
+            htc.append(rcopy(
+                turned.at[ht_rows(cc, zz, yy), :],
+                htall.at[pl.ds(zz * shard, shard), pl.ds(k * tok, tok)],
+                hts.at[k - 1, zz], htr.at[k - 1, zz], to,
+            ))
+            send(htc[-1])
 
     own = pl.multiple_of((c * 8 + l) * shard, shard)
     qb = cols // sc_ref.shape[1]
@@ -179,10 +189,10 @@
 
     for ch in range(1, CHUNKS):
         ogall[ch, 0:tok, :] = og_ref[:, ch * cw:(ch + 1) * cw]
-    send(ogy(1))
     for ch in range(CHUNKS):
         send(ogc(ch))
-    htall[:, 0:tok] = ht_ref[c, y]
+    for zz in range(4):
+        htall[zz * shard:(zz + 1) * shard, 0:tok] = turned[ht_rows(c, zz, y), :]
     core_send(z, y, 0)
     core_send(z, y, 1)
 
@@ -202,8 +212,8 @@
         if ch + 2 < CHUNKS:
             send(ogy(ch + 2))
         if ch == 0:
-            for k in (1, 2, 3):
-                htc[k].wait_recv()
+            for copy in htc:
+                copy.wait_recv()
         ogc(ch).wait_recv()
         ogd(ch).wait_recv()
         term = jnp.dot(htall[...], ogall[ch], preferred_element_type=jnp.float32)
@@ -269,41 +279,42 @@
                 arrive(zz, yy, hh, cn, cs.at[0], to_c)
 
     z_step(pair, 2, to_inner)
+    send(ogy(1))
     z_step(inner, 3, to_pair)
     grads(0)
     z_step(outer, 4, to_pair)
     grads(1)
-    passed_on(0)
+    y_send(z)
     grads(2)
-    y_send(z)
     y_send(pair)
-    passed_on(1)
+    y_send(inner)
     grads(3)
-    y_send(inner)
     y_send(outer)
-    passed_on(2)
     c_step(pair, y)
     c_step(inner, y)
     c_step(outer, y)
+    passed_on(0)
     b_step(z)
-    passed_on(3)
     b_step(pair)
+    passed_on(1)
     c_step(z, yn)
     b_step(inner)
     c_step(pair, yn)
+    apply(c, side, True)
+    passed_on(2)
     b_step(outer)
-    apply(c, side, True)
+    c_step(inner, yn)
+    passed_on(3)
     core_arrive(z)
     core_arrive(pair)
     apply(cn, side, False)
-    c_step(inner, yn)
     c_step(outer, yn)
-    for ch in range(CHUNKS):
-        finish(ch)
     apply(c, 1 - side, False)
     core_arrive(inner)
     core_arrive(outer)
     apply(cn, 1 - side, False)
+    for ch in range(CHUNKS):
+        finish(ch)
     proj_ref[...] = acc[...].astype(jnp.bfloat16)
 
     for copy in started:
@@ -324,8 +335,6 @@
     shard = quant_values.shape[0]
     cw = cols // CHUNKS
     token_count = tok * lax.axis_size("node") * lax.axis_size("local")
-    turned = head_outputs.T.reshape(2, 4, 2, shard, tok).transpose(0, 2, 1, 3, 4)
-    turned = turned.reshape(2, 2, 4 * shard, tok)
     vmem = pl.BlockSpec(memory_space=pltpu.VMEM)
     bf16, f32 = jnp.bfloat16, jnp.float32
     dma = pltpu.SemaphoreType.DMA
@@ -336,10 +345,11 @@
             jax.ShapeDtypeStruct((tok, rows), bf16),
             jax.ShapeDtypeStruct((shard, cols), f32),
         ),
-        in_specs=[vmem] * 5,
+        in_specs=[vmem] * 4,
         out_specs=(vmem,) * 3,
         scratch_shapes=[
             pltpu.VMEM((rows, cols), bf16),
+            pltpu.VMEM((rows, tok), bf16),
             pltpu.VMEM((4 * shard, 4 * tok), bf16),
             pltpu.VMEM((CHUNKS, 4 * tok, cw), bf16),
             pltpu.VMEM((CHUNKS, 4, shard, cw), f32),
@@ -348,7 +358,7 @@
             pltpu.VMEM((CHUNKS, shard, cw), bf16),
             pltpu.VMEM((CHUNKS, 2, shard, cw), bf16),
             pltpu.VMEM((tok, cols), f32),
-            dma((3,)), dma((3,)),
+            dma((3, 4)), dma((3, 4)),
             dma((CHUNKS,)), dma((CHUNKS,)),
             dma((CHUNKS,)), dma((CHUNKS,)),
             dma((CHUNKS,)), dma((CHUNKS,)),
@@ -361,7 +371,7 @@
         cost_estimate=pl.CostEstimate(
             flops=6 * tok * rows * cols, bytes_accessed=8 * tok * cols, transcendentals=0
         ),
-    )(head_outputs, out_grads, turned, quant_values, block_scales)
+    )(head_outputs, out_grads, quant_values, block_scales)
 
 
 def per_device_plain(head_outputs, out_grads, quant_values, block_scales):
@@ -385,6 +395,7 @@
         and shard % 32 == 0
         and (4 * shard) % 128 == 0
         and head_outputs.shape[0] % 256 == 0
+        and head_outputs.shape[1] % 256 == 0
         and out_grads.shape[1] % (CHUNKS * 128) == 0
     )
     if fits:

time: 138 us -> 117 us (0.85)
  the two profiles are of different devices: /device:TPU:8 before, /device:TPU:0 now
where the time goes in v2:
time: 117 us
  Pallas kernels  109 us (93%)
  local copies, waits for them, and re-layouts  7.06 us (6%)
    pallas_call x1, Pallas kernels, per_device_fused(): pl.pallas_call(functools.partial(fused_kernel, token_count ** (-0.5)), ou...  109 us
    unnamed x8, local copies, waits for them, and re-layouts  7.06 us

profile of v2, /device:TPU:0, one launch (start us, length us, event | category | flops | bytes accessed | tf_op | source)
XLA Modules:
  0.0 117.0 jit_solution(13707851905127543523)
XLA Ops:
  0.6 1.4 %copy.7.sc_ref = bf16[160,10]{1,0:T(8,128)(2,1)} copy(bf16[160,10]{0,1:T(8,128)(2,1)} %param.7) | data formatting | bytes 6400 | tf_op args[3]
  2.1 109.2 %shard_map.67 = (bf16[256,2560]{1,0:T(8,128)(2,1)}, bf16[256,2560]{1,0:T(8,128)(2,1)}, f32[160,2560]{1,0:T(8,128)}) custom-call(bf16[256,2560]{1,0:T(8,128)(2,1)} %ho_ref.1, bf16[256,2560]{1,0:T(8,128)(2,1)} %og_ref.1, bf16[160,2560]{1,0:T(8,128)(2,1)} %qv_ref.1, bf16[160,10]{1,0:T(8,128)(2,1)} %copy.7.sc_ref), custom_call_target="tpu_custom_call" | custom-call | flops 10066329600 | bytes 5242880 | tf_op jit(solution)/shard_map/pallas_call | solution.py:341
  111.3 0.0 copy-start.1
  111.3 2.6 %copy.11 = bf16[256,2560]{1,0:T(8,128)(2,1)} copy(bf16[256,2560]{1,0:T(8,128)(2,1)} %get-tuple-element.6) | data formatting | bytes 2621440
  113.9 0.0 copy-done.1
  113.9 0.0 copy-start
  113.9 1.1 copy.12
  114.9 0.8 copy-done
  115.8 1.2 copy.13
Async XLA Ops:
  111.3 2.6 %copy-start.1 = (bf16[256,2560]{1,0:T(8,128)(2,1)S(1)}, bf16[256,2560]{1,0:T(8,128)(2,1)}, u32[]{:S(2)}) copy-start(bf16[256,2560]{1,0:T(8,128)(2,1)} %get-tuple-element.7) | copy-start | bytes 3932164
  113.9 1.9 %copy-start = (f32[160,2560]{1,0:T(8,128)S(1)}, f32[160,2560]{1,0:T(8,128)}, u32[]{:S(2)}) copy-start(f32[160,2560]{1,0:T(8,128)} %get-tuple-element.8) | copy-start | bytes 4915204

commit v3 on v2

--- a/solution.py
+++ b/solution.py
@@ -172,12 +172,15 @@
             send(htc[-1])
 
     own = pl.multiple_of((c * 8 + l) * shard, shard)
-    qb = cols // sc_ref.shape[1]
-    for b in range(sc_ref.shape[1]):
-        w[pl.ds(own, shard), b * qb:(b + 1) * qb] = (
-            qv_ref[:, b * qb:(b + 1) * qb].astype(jnp.float32)
-            * sc_ref[:, b:b + 1].astype(jnp.float32)
-        ).astype(jnp.bfloat16)
+    blocks = sc_ref.shape[0]
+    qb = cols // blocks
+    hot = lax.broadcasted_iota(jnp.int32, (blocks, cols), 1) // qb
+    hot = hot == lax.broadcasted_iota(jnp.int32, (blocks, cols), 0)
+    factor = lax.dot_general(
+        sc_ref[...].astype(jnp.float32).T.astype(jnp.bfloat16), hot.astype(jnp.bfloat16),
+        (((1,), (0,)), ((), ())), preferred_element_type=jnp.float32,
+    )
+    w[pl.ds(own, shard), :] = (qv_ref[...].astype(jnp.float32) * factor).astype(jnp.bfloat16)
 
     send(piece(z, y, x, c, zs.at[0], to_pair))
 
@@ -304,17 +307,19 @@
     passed_on(2)
     b_step(outer)
     c_step(inner, yn)
-    passed_on(3)
     core_arrive(z)
     core_arrive(pair)
     apply(cn, side, False)
+    passed_on(3)
+    finish(0)
+    finish(1)
     c_step(outer, yn)
+    finish(2)
     apply(c, 1 - side, False)
     core_arrive(inner)
     core_arrive(outer)
     apply(cn, 1 - side, False)
-    for ch in range(CHUNKS):
-        finish(ch)
+    finish(3)
     proj_ref[...] = acc[...].astype(jnp.bfloat16)
 
     for copy in started:
@@ -371,7 +376,7 @@
         cost_estimate=pl.CostEstimate(
             flops=6 * tok * rows * cols, bytes_accessed=8 * tok * cols, transcendentals=0
         ),
-    )(head_outputs, out_grads, quant_values, block_scales)
+    )(head_outputs, out_grads, quant_values, block_scales.T)
 
 
 def per_device_plain(head_outputs, out_grads, quant_values, block_scales):

time: 117 us -> 116 us (level)
  local copies, waits for them, and re-layouts: 7.06 us -> 5.63 us
    unnamed x8 -> x7, local copies, waits for them, and re-layouts: 7.06 us -> 5.63 us
where the time goes in v3:
time: 116 us; the launch traced here: 115 us
  Pallas kernels  109 us (94%)
  local copies, waits for them, and re-layouts  5.63 us (5%)
    pallas_call x1, Pallas kernels, per_device_fused(): pl.pallas_call(functools.partial(fused_kernel, token_count ** (-0.5)), ou...  109 us
    unnamed x7, local copies, waits for them, and re-layouts  5.63 us

profile of v3, /device:TPU:0, one launch (start us, length us, event | category | flops | bytes accessed | tf_op | source)
XLA Modules:
  0.0 115.4 jit_solution(15844193370687044770)
XLA Ops:
  0.6 109.1 %shard_map.67 = (bf16[256,2560]{1,0:T(8,128)(2,1)}, bf16[256,2560]{1,0:T(8,128)(2,1)}, f32[160,2560]{1,0:T(8,128)}) custom-call(bf16[256,2560]{1,0:T(8,128)(2,1)} %ho_ref.1, bf16[256,2560]{1,0:T(8,128)(2,1)} %og_ref.1, bf16[160,2560]{1,0:T(8,128)(2,1)} %qv_ref.1, bf16[10,160]{1,0:T(8,128)(2,1)} %bitcast.1), custom_call_target="tpu_custom_call" | custom-call | flops 10066329600 | bytes 5242880 | tf_op jit(solution)/shard_map/pallas_call | solution.py:346
  109.8 0.0 copy-start.1
  109.8 2.6 %copy.10 = bf16[256,2560]{1,0:T(8,128)(2,1)} copy(bf16[256,2560]{1,0:T(8,128)(2,1)} %get-tuple-element.6) | data formatting | bytes 2621440
  112.3 0.0 copy-done.1
  112.3 0.0 copy-start
  112.3 1.1 copy.11
  113.4 0.8 copy-done
  114.2 1.2 %copy.12 = f32[160,2560]{1,0:T(8,128)} copy(f32[160,2560]{1,0:T(8,128)S(1)} %copy-done) | data formatting | bytes 3276800
Async XLA Ops:
  109.8 2.6 %copy-start.1 = (bf16[256,2560]{1,0:T(8,128)(2,1)S(1)}, bf16[256,2560]{1,0:T(8,128)(2,1)}, u32[]{:S(2)}) copy-start(bf16[256,2560]{1,0:T(8,128)(2,1)} %get-tuple-element.7) | copy-start | bytes 3932164
  112.3 1.9 %copy-start = (f32[160,2560]{1,0:T(8,128)S(1)}, f32[160,2560]{1,0:T(8,128)}, u32[]{:S(2)}) copy-start(f32[160,2560]{1,0:T(8,128)} %get-tuple-element.8) | copy-start | bytes 4915204

commit v4 on v3

--- a/solution.py
+++ b/solution.py
@@ -248,7 +248,7 @@
     quarter = 4 * shard
     tile = cw
 
-    def apply(cc, ss, first):
+    def apply(cc, ss, first, last=False):
         row = pl.multiple_of((cc * 2 + ss) * quarter, 128)
         left = ho_ref[:, pl.ds(row, quarter)]
 
@@ -257,6 +257,8 @@
             term = jnp.dot(left, w[pl.ds(row, quarter), at], preferred_element_type=jnp.float32)
             if first:
                 acc[:, at] = term
+            elif last:
+                proj_ref[:, at] = (acc[:, at] + term).astype(jnp.bfloat16)
             else:
                 acc[:, at] += term
             return carry
@@ -318,9 +320,8 @@
     apply(c, 1 - side, False)
     core_arrive(inner)
     core_arrive(outer)
-    apply(cn, 1 - side, False)
+    apply(cn, 1 - side, False, True)
     finish(3)
-    proj_ref[...] = acc[...].astype(jnp.bfloat16)
 
     for copy in started:
         copy.wait_send()

time: 116 us -> 115 us (level)
  no operation moved by 1% of the time
where the time goes in v4:
time: 115 us
  Pallas kernels  109 us (95%)
  local copies, waits for them, and re-layouts  5.63 us (5%)
    pallas_call x1, Pallas kernels, per_device_fused(): pl.pallas_call(functools.partial(fused_kernel, token_count ** (-0.5)), ou...  109 us
    unnamed x7, local copies, waits for them, and re-layouts  5.63 us

profile of v4, /device:TPU:0, one launch (start us, length us, event | category | flops | bytes accessed | tf_op | source)
XLA Modules:
  0.0 115.3 jit_solution(6306440230860657137)
XLA Ops:
  0.6 109.0 %shard_map.67 = (bf16[256,2560]{1,0:T(8,128)(2,1)}, bf16[256,2560]{1,0:T(8,128)(2,1)}, f32[160,2560]{1,0:T(8,128)}) custom-call(bf16[256,2560]{1,0:T(8,128)(2,1)} %ho_ref.1, bf16[256,2560]{1,0:T(8,128)(2,1)} %og_ref.1, bf16[160,2560]{1,0:T(8,128)(2,1)} %qv_ref.1, bf16[10,160]{1,0:T(8,128)(2,1)} %bitcast.1), custom_call_target="tpu_custom_call" | custom-call | flops 10066329600 | bytes 5242880 | tf_op jit(solution)/shard_map/pallas_call | solution.py:347
  109.6 0.0 copy-start.1
  109.6 2.6 %copy.10 = bf16[256,2560]{1,0:T(8,128)(2,1)} copy(bf16[256,2560]{1,0:T(8,128)(2,1)} %get-tuple-element.6) | data formatting | bytes 2621440
  112.2 0.0 copy-done.1
  112.2 0.0 copy-start
  112.2 1.1 copy.11
  113.3 0.8 copy-done
  114.1 1.2 %copy.12 = f32[160,2560]{1,0:T(8,128)} copy(f32[160,2560]{1,0:T(8,128)S(1)} %copy-done) | data formatting | bytes 3276800
Async XLA Ops:
  109.6 2.6 %copy-start.1 = (bf16[256,2560]{1,0:T(8,128)(2,1)S(1)}, bf16[256,2560]{1,0:T(8,128)(2,1)}, u32[]{:S(2)}) copy-start(bf16[256,2560]{1,0:T(8,128)(2,1)} %get-tuple-element.7) | copy-start | bytes 3932164
  112.2 1.9 %copy-start = (f32[160,2560]{1,0:T(8,128)S(1)}, f32[160,2560]{1,0:T(8,128)}, u32[]{:S(2)}) copy-start(f32[160,2560]{1,0:T(8,128)} %get-tuple-element.8) | copy-start | bytes 4915204
